TPU v7x, 32 devices: a whole 2x2x4 slice. The times are simulated.
32 devices in a mesh: ka: 4 (over y, x), pw: 8 (over z, core).
Axes of the slice: x: 2, y: 2, z: 4, core: 2. Of those that a mesh axis runs over, the one named last changes fastest.
Arguments:
- states_re: bfloat16 [8, 512, 32768], P('ka', None, 'pw'), may hold values from -0.016572815 to 0.016572815
- states_im: bfloat16 [8, 512, 32768], P('ka', None, 'pw'), may hold values from -0.016572815 to 0.016572815
Outputs:
- wilson_lines: float32 [8, 512, 2, 512], P('ka', 'pw')
All inputs are finite; a program needn't handle non-finite values.
Results may differ from a plain program's by a relative error of at most 0.0003.
Values may be sent and summed in bfloat16 or wider, within the bound.
No kernel may reach another device: no remote copies, remote signals or barrier semaphores. Data moves between devices by JAX's collectives and lax.ppermute only.
A program may use at most 128 MiB of HBM per device.

v0:
```python
import functools

import jax
import jax.numpy as jnp
from jax import lax
from jax.experimental import pallas as pl
from jax.experimental.pallas import tpu as pltpu
from jax.sharding import PartitionSpec as P

VMEM_LIMIT = 40 * 1024 * 1024


def halves_of(value):
    high = value.astype(jnp.bfloat16)
    return high, (value - high.astype(jnp.float32)).astype(jnp.bfloat16)


def dot(left, right, across=0):
    return lax.dot_general(left, right, (((1,), (across,)), ((), ())), preferred_element_type=jnp.float32)


def turned(value):
    width = value.shape[1] // 2
    return jnp.concatenate([-value[:, width:], value[:, :width]], 1)


def margin_kernel(steps, pieces, with_left, by_core, *refs):
    refs = list(refs)
    core = refs.pop(0) if by_core else None
    own_re, own_im = refs[:2]
    real_part = jnp.concatenate([ref[...] for ref in refs[2 : 2 + pieces]], 0)
    imag_part = jnp.concatenate([ref[...] for ref in refs[2 + pieces : 2 + 2 * pieces]], 0)
    refs = refs[2 + 2 * pieces :]
    left_high, left_low = refs[:2] if with_left else (None, None)
    outs, total = refs[2 if with_left else 0 : -1], refs[-1]
    step = pl.program_id(0)
    other = jnp.concatenate([jnp.concatenate([real_part, imag_part], 1), jnp.concatenate([imag_part, -real_part], 1)], 0)
    term = dot(jnp.concatenate([own_re[...], own_im[...]], 1), other, 1)

    @pl.when(step == 0)
    def _():
        total[...] = term

    @pl.when(step > 0)
    def _():
        total[...] += term

    @pl.when(step == steps - 1)
    def _():
        if with_left:
            bands = left_high.shape[0]
            value = total[...]
            product = jnp.zeros_like(value)
            for first, factor in ((0, value), (bands, turned(value))):
                high, low = halves_of(factor)
                columns = slice(first, first + bands)
                product += dot(left_high[:, columns], high)
                product += dot(left_high[:, columns], low)
                product += dot(left_low[:, columns], high)
            total[...] = product
        if by_core:
            mine, theirs = outs
            rows = mine.shape[1]
            for chip in range(mine.shape[0]):
                for out, which in ((mine, core[0]), (theirs, 1 - core[0])):
                    first = pl.multiple_of((2 * chip + which) * rows, rows)
                    out[chip] = total[pl.ds(first, rows), :]
        else:
            outs[0][...] = total[...]


def margin_section(states, kpoint, others=None, left=None, core=None):
    _, bands, waves = states[0].shape
    depth = min(1024, waves)
    steps = waves // depth
    own = pl.BlockSpec((None, bands, depth), lambda step: (kpoint, 0, step))
    if others is None:
        width = bands
        other_specs = [pl.BlockSpec((None, bands, depth), lambda step: (kpoint + 1, 0, step))] * 2
        others = states
    else:
        packs = [other if isinstance(other, tuple) else (other, other) for other in others]
        apart = [isinstance(other, tuple) for other in others]
        widths = [pack[0].shape[0] // (1 if one else 2) for pack, one in zip(packs, apart)]
        width = sum(widths)
        other_specs = [pl.BlockSpec((one, depth), lambda step: (0, step)) for one in widths]
        for one, alone in zip(widths, apart):
            other_specs.append(pl.BlockSpec((one, depth), functools.partial(lambda row, step: (row, step), 0 if alone else 1)))
        others = [pack[0] for pack in packs] + [pack[1] for pack in packs]
    operands, specs = [*states, *others], [own, own, *other_specs]
    if left is not None:
        operands += left
        specs += [pl.BlockSpec((bands, 2 * bands), lambda step: (0, 0))] * 2
    if core is not None:
        operands = [core, *operands]
        specs = [pl.BlockSpec(memory_space=pltpu.SMEM), *specs]
        chips = lax.axis_size("pw") // 2
        shape = (chips, bands // (2 * chips), 2 * width)
        out_shape = [jax.ShapeDtypeStruct(shape, jnp.float32)] * 2
        out_specs = [pl.BlockSpec(shape, lambda step: (0, 0, 0))] * 2
    else:
        out_shape = jax.ShapeDtypeStruct((bands, 2 * width), jnp.float32)
        out_specs = pl.BlockSpec((bands, 2 * width), lambda step: (0, 0))
    return pl.pallas_call(
        functools.partial(margin_kernel, steps, len(other_specs) // 2, left is not None, core is not None),
        grid=(steps,),
        in_specs=specs,
        out_specs=out_specs,
        out_shape=out_shape,
        scratch_shapes=[pltpu.VMEM((bands, 2 * width), jnp.float32)],
        compiler_params=pltpu.CompilerParams(vmem_limit_bytes=VMEM_LIMIT),
        cost_estimate=pl.CostEstimate(flops=0, bytes_accessed=0, transcendentals=0),
    )(*operands)


def split_kernel(value, high, low):
    high[...], low[...] = halves_of(value[...])


def split(value):
    return pl.pallas_call(
        split_kernel,
        out_shape=[jax.ShapeDtypeStruct(value.shape, jnp.bfloat16)] * 2,
        compiler_params=pltpu.CompilerParams(vmem_limit_bytes=VMEM_LIMIT),
    )(value)


def whole_rows(term):
    if len(term) == 1 and len(term[0].shape) == 3:
        rows = term[0][...]
        return jnp.concatenate([rows[0], rows[1]], 0)
    widths = [ref.shape[1] // 2 for ref in term]
    reals = [ref[:, :width] for ref, width in zip(term, widths)]
    imags = [ref[:, width:] for ref, width in zip(term, widths)]
    return jnp.concatenate([jnp.concatenate(reals, 1), jnp.concatenate(imags, 1)], 0)


def join_kernel(place, *refs):
    *refs, out = refs
    pairs = len(refs) // 2
    total, first = out.shape[1] // 2, 0
    for mine, theirs in zip(refs[:pairs], refs[pairs:]):
        chips, rows, width = mine.shape
        for chip in range(chips):
            turn = lax.rem(place[0] - chip + chips, chips)
            one, other = mine[turn], theirs[turn]
            for core in (0, 1):
                high, low = halves_of(jnp.where(place[1] == core, one, other))
                where = slice((2 * chip + core) * rows, (2 * chip + core + 1) * rows)
                out[where, first : first + width] = high
                out[where, total + first : total + first + width] = low
        first += width


def joined(place, mine, theirs):
    chips, rows, _ = mine[0].shape
    columns = sum(one.shape[2] for one in mine)
    return pl.pallas_call(
        join_kernel,
        in_specs=[pl.BlockSpec(memory_space=pltpu.SMEM)] + [pl.BlockSpec()] * (2 * len(mine)),
        out_specs=pl.BlockSpec(memory_space=pltpu.VMEM),
        out_shape=jax.ShapeDtypeStruct((2 * chips * rows, 2 * columns), jnp.bfloat16),
        compiler_params=pltpu.CompilerParams(vmem_limit_bytes=VMEM_LIMIT),
        cost_estimate=pl.CostEstimate(flops=0, bytes_accessed=0, transcendentals=0),
    )(place, *mine, *theirs)


def times_into(out, by_row, both, high, pieces):
    count = high.shape[0] // 2
    first = 0
    for piece_high, piece_low in pieces:
        product = dot(both, piece_high)
        product = product[: 2 * count] + product[2 * count :] + dot(high, piece_low)
        width = product.shape[1] // 2
        columns = slice(first, first + width)
        real_part = product[:count, :width] - product[count:, width:]
        imag_part = product[:count, width:] + product[count:, :width]
        if by_row:
            out[:, 0, columns] = real_part
            out[:, 1, columns] = imag_part
        else:
            out[0, :, columns] = real_part
            out[1, :, columns] = imag_part
        first += width


def span_pieces(span, widths):
    total, first = span.shape[1] // 2, 0
    for width in widths:
        yield span[:, first : first + 2 * width], span[:, total + first : total + first + 2 * width]
        first += 2 * width


def split_rows(flat):
    high, low = halves_of(flat)
    return jnp.concatenate([high, low], 0), high


def hop_kernel(widths, part, *refs):
    *term, before, span, line, after_rows = refs
    flat = whole_rows(term)
    count = flat.shape[0] // 2
    times_into(line, False, *split_rows(flat), span_pieces(span, widths))
    where = slice(part * count, (part + 1) * count)
    after_rows[0] = before[0, where, :] + flat[:count]
    after_rows[1] = before[1, where, :] + flat[count:]


def hop(term, before, part, count, span, widths):
    shape = (2, count, before.shape[2])
    return pl.pallas_call(
        functools.partial(hop_kernel, widths, part),
        out_shape=[jax.ShapeDtypeStruct(shape, jnp.float32)] * 2,
        compiler_params=pltpu.CompilerParams(vmem_limit_bytes=VMEM_LIMIT),
        cost_estimate=pl.CostEstimate(flops=0, bytes_accessed=0, transcendentals=0),
    )(*term, before, span)


def first_hop_kernel(widths, parts, *refs):
    refs, lines, after_rows = refs[: -parts - 1], refs[-parts - 1 : -1], refs[-1]
    *term, before, span = refs
    flat = whole_rows(term)
    count = flat.shape[0] // 2
    after_rows[0] = before[0] + flat[:count]
    after_rows[1] = before[1] + flat[count:]
    step = count // parts
    for part, line in enumerate(lines):
        where = slice(part * step, (part + 1) * step)
        some = jnp.concatenate([flat[:count][where], flat[count:][where]], 0)
        times_into(line, False, *split_rows(some), span_pieces(span, widths))


def first_hop(term, before, span, widths, parts):
    _, count, bands = before.shape
    shapes = [(2, count // parts, bands)] * parts + [before.shape]
    return pl.pallas_call(
        functools.partial(first_hop_kernel, widths, parts),
        out_shape=[jax.ShapeDtypeStruct(shape, jnp.float32) for shape in shapes],
        compiler_params=pltpu.CompilerParams(vmem_limit_bytes=VMEM_LIMIT),
        cost_estimate=pl.CostEstimate(flops=0, bytes_accessed=0, transcendentals=0),
    )(*term, before, span)


def last_kernel(widths, parts, *refs):
    before, *refs = refs
    received, (*margins, span, out) = refs[:parts], refs[parts:]
    for part, ref in enumerate(received):
        count = ref.shape[1]
        where = slice(part * count, (part + 1) * count)
        reals, imags = before[0, where, :] + ref[0], before[1, where, :] + ref[1]
        both, high = split_rows(jnp.concatenate([reals, imags], 0))
        for i, margin in enumerate(margins):
            times_into(out.at[i, where], True, both, high, [halves_of(margin[...])])
        times_into(out.at[len(margins), where], True, both, high, span_pieces(span, widths))


def last_lines(before, received, span, widths, margins):
    _, count, bands = before.shape
    return pl.pallas_call(
        functools.partial(last_kernel, widths, len(received)),
        out_shape=jax.ShapeDtypeStruct((len(margins) + 1, count, 2, bands), jnp.float32),
        compiler_params=pltpu.CompilerParams(vmem_limit_bytes=VMEM_LIMIT),
        cost_estimate=pl.CostEstimate(flops=0, bytes_accessed=0, transcendentals=0),
    )(before, *received, *margins, span)


def complex_dot(left, right):
    bands = left.shape[0]
    dots = [jnp.dot(left[:, i : i + bands], right, precision=lax.Precision.HIGH) for i in (0, bands)]
    return jnp.concatenate(
        [dots[0][:, :bands] - dots[1][:, bands:], dots[0][:, bands:] + dots[1][:, :bands]], 1
    )


def packed(states, kpoint, first, width):
    return jnp.concatenate([s[kpoint, first : first + width] for s in states], 0)


def after(value, earlier):
    return lax.optimization_barrier((value, earlier))[0]


def other_core(block):
    size = lax.axis_size("pw")
    return lax.ppermute(block, "pw", [(i, i ^ 1) for i in range(size)])


def other_chip(block, distance):
    size = lax.axis_size("pw")
    return lax.ppermute(block, "pw", [(i, (i + 2 * distance) % size) for i in range(size)])


def sum_to_rows(mine, theirs):
    chips = mine.shape[0]
    chip = lax.axis_index("pw") // 2
    half = mine + other_core(theirs)

    def block(place):
        return lax.dynamic_index_in_dim(half, place % chips, 0, keepdims=False)

    received = [other_chip(block(chip + d), d) for d in range(1, chips)]
    return sum(received, block(chip))


def rows_to_core(rows):
    chips = lax.axis_size("pw") // 2
    return jnp.stack([rows] + [other_chip(rows, d) for d in range(1, chips)], 0)


def shards(states_re, states_im):
    kcount, bands, _ = states_re.shape
    ka_width = lax.axis_size("ka")
    pw_width = lax.axis_size("pw")
    band_rows = bands // pw_width
    ka_place = lax.axis_index("ka")
    first_band = lax.axis_index("pw") * band_rows
    core = (lax.axis_index("pw") % 2).reshape(1).astype(jnp.int32)
    place = jnp.stack([lax.axis_index("pw") // 2, lax.axis_index("pw") % 2]).astype(jnp.int32)
    quarter = bands // 4
    widths = [2 * quarter, quarter, quarter]
    firsts = [sum(widths[:i]) for i in range(len(widths))]
    to_previous = [(i, (i - 1) % ka_width) for i in range(ka_width)]
    blocks = [tuple(state[0, : widths[0]] for state in (states_re, states_im))]
    blocks += [packed((states_re, states_im), 0, first, width) for first, width in zip(firsts[1:], widths[1:])]

    def send(number, *earlier):
        return lax.ppermute(after(blocks[number], earlier) if earlier else blocks[number], "ka", to_previous)

    arrivals = [send(0)]
    states = after((states_re, states_im), blocks[0])
    last = kcount - 1
    terms = [margin_section(states, k) for k in range(last)]
    arrivals.append(send(1, terms))
    own_margins = [lax.psum(term, "pw") for term in terms]
    before = own_margins[0]
    for k in range(1, last):
        before = own_margins[k] = complex_dot(before, own_margins[k])
    left = split(after(before, arrivals[0]))

    rows, halves, swapped = [], [], []
    ready = None
    for number in range(len(widths)):
        piece = arrivals[number]
        final = number == len(widths) - 1
        if final:
            reals = [one[:, : one.shape[1] // 2] for one in rows]
            imags = [one[:, one.shape[1] // 2 :] for one in rows]
            ready = lax.ppermute(after(jnp.concatenate(reals + imags, 1), (piece, swapped)), "ka", [(0, 1)])
        if halves:
            piece = after(piece, halves[-1])
        mine, theirs = margin_section(states, last, [piece], left, core)
        if number == 0:
            arrivals.append(send(2, arrivals[0], mine))
        rows.append(sum_to_rows(mine, after(theirs, ready) if final else theirs))
        half = rows_to_core(rows[-1])
        if final:
            received = [ready, lax.ppermute(rows[-1], "ka", [(0, 1)])]
            half = after(half, received[-1])
        halves.append(half)
        swapped.append(other_core(half))
    span = joined(place, halves, swapped)

    row_index = lax.broadcasted_iota(jnp.int32, (band_rows, bands), 0) + first_band
    col_index = lax.broadcasted_iota(jnp.int32, (band_rows, bands), 1)
    eye_real = jnp.where((row_index == col_index) & (ka_place == 0), 1.0, 0.0).astype(jnp.float32)
    start = jnp.stack([eye_real, jnp.zeros_like(eye_real)], 0)
    parts = 2
    *lines, start = first_hop(received, start, span, widths, parts)
    for number in range(1, ka_width - 1):
        received = [lax.ppermute(line, "ka", [(number, number + 1)]) for line in lines]
        if number < ka_width - 2:
            handed = [hop([one], start, part, band_rows // parts, span, widths) for part, one in enumerate(received)]
            lines = [line for line, _ in handed]
            start = jnp.concatenate([rows for _, rows in handed], 1)

    return last_lines(start, received, span, widths, own_margins)


def solution(mesh):
    in_specs = (P("ka", None, "pw"), P("ka", None, "pw"))
    out_specs = P("ka", "pw", None, None)
    return jax.shard_map(shards, mesh=mesh, in_specs=in_specs, out_specs=out_specs, check_vma=False)
```

profile of v0, /device:TPU:6, one launch (start us, length us, event | category | flops | bytes accessed | tf_op | source)
XLA Modules:
  0.0 250.8 jit_solution(1652740499272386993)
XLA Ops:
  6.5 3.4 %slice_bitcast_fusion = bf16[256,4096]{1,0:T(8,128)(2,1)} fusion(bf16[2,512,4096]{2,1,0:T(8,128)(2,1)} %refs_2_.3), kind=kLoop, calls=%fused_computation.2 | loop fusion | bytes 4194304 | tf_op jit(solution)/shard_map/squeeze | solution.py:323
  10.4 3.1 %slice_bitcast_fusion.1 = bf16[256,4096]{1,0:T(8,128)(2,1)} fusion(bf16[2,512,4096]{2,1,0:T(8,128)(2,1)} %refs_1_.3), kind=kLoop, calls=%fused_computation.3 | loop fusion | bytes 4194304 | tf_op jit(solution)/shard_map/squeeze | solution.py:323
  13.6 1.4 collective-permute-start
  15.0 2.7 %slice_bitcast_fusion.3 = (bf16[128,4096]{1,0:T(8,128)(2,1)}, bf16[128,4096]{1,0:T(8,128)(2,1)S(1)}) fusion(bf16[2,512,4096]{2,1,0:T(8,128)(2,1)} %refs_1_.3), kind=kLoop, calls=%fused_computation.5 | loop fusion | bytes 4194304 | tf_op jit(solution)/shard_map/squeeze | solution.py:276
  17.8 13.6 %shard_map.28 = f32[512,1024]{1,0:T(8,128)} custom-call(bf16[2,512,4096]{2,1,0:T(8,128)(2,1)S(1)} %copy-done, bf16[2,512,4096]{2,1,0:T(8,128)(2,1)} %refs_2_.3, bf16[2,512,4096]{2,1,0:T(8,128)(2,1)S(1)} %copy-done, bf16[2,512,4096]{2,1,0:T(8,128)(2,1)} %refs_2_.3), custom_call_target="tpu_custom_call" | custom-call | tf_op jit(solution)/shard_map/pallas_call | solution.py:104
  31.3 2.7 %slice_bitcast_fusion.2 = (bf16[128,4096]{1,0:T(8,128)(2,1)}, bf16[128,4096]{1,0:T(8,128)(2,1)S(1)}) fusion(bf16[2,512,4096]{2,1,0:T(8,128)(2,1)} %refs_2_.3), kind=kLoop, calls=%fused_computation.4 | loop fusion | bytes 4194304 | tf_op jit(solution)/shard_map/squeeze | solution.py:276
  34.1 1.5 pad_maximum_fusion
  36.1 66.0 %all-reduce.3.cloned.1.call-done.value.refs_3_ = f32[512,1024]{1,0:T(8,128)} async-done(((f32[512,1024]{1,0:T(8,128)}), f32[512,1024]{1,0:T(8,128)}) %all-reduce.3.cloned.1.call-update) | async-done | bytes 2097168 | tf_op jit(solution)/shard_map/psum | solution.py:334
  102.1 1.4 copy-done.4
  104.6 1.6 copy-done.2
  106.5 1.3 copy-done.5
  107.8 9.5 %shard_map.30 = (f32[4,64,512]{2,1,0:T(8,128)S(1)}, f32[4,64,512]{2,1,0:T(8,128)S(1)}) custom-call(s32[1]{0:T(128)} %bitcast.refs_0_, bf16[2,512,4096]{2,1,0:T(8,128)(2,1)} %refs_1_.3, bf16[2,512,4096]{2,1,0:T(8,128)(2,1)} %refs_2_.3, bf16[256,4096]{1,0:T(8,128)(2,1)} %collective-permute-done.refs_3_, bf16[256,4096]{1,0:T(8,128)(2,1)S(1)} %copy-done.5, ...), custom_call_target="tpu_custom_call" | custom-call | tf_op jit(solution)/shard_map/pallas_call | solution.py:104
  117.4 3.1 %pad_maximum_fusion.1 = bf16[256,4096]{1,0:T(8,128)(2,1)} fusion(bf16[128,4096]{1,0:T(8,128)(2,1)} %get-tuple-element.57, bf16[128,4096]{1,0:T(8,128)(2,1)} %get-tuple-element.55), kind=kLoop, calls=%fused_computation.1 | loop fusion | flops 4194304 | bytes 4194304 | tf_op jit(solution)/shard_map/concatenate | solution.py:276
  120.6 1.1 add.111
  121.7 1.6 collective-permute-start.3
  123.4 2.2 collective-permute-start.5
  126.4 3.5 %collective-permute-done.3 = f32[64,512]{1,0:T(8,128)S(1)} collective-permute-done((f32[64,512]{1,0:T(8,128)S(1)}, f32[64,512]{1,0:T(8,128)S(1)}, u32[]{:S(2)}, u32[]{:S(2)}) %collective-permute-start.3) | collective-permute-done | bytes 131104 | tf_op jit(solution)/shard_map/ppermute | solution.py:290
  129.9 1.8 collective-permute-done.5
  131.7 6.2 %collective-permute-done.4 = f32[64,512]{1,0:T(8,128)S(1)} collective-permute-done((f32[64,512]{1,0:T(8,128)S(1)}, f32[64,512]{1,0:T(8,128)S(1)}, u32[]{:S(2)}, u32[]{:S(2)}) %collective-permute-start.4) | collective-permute-done | bytes 131104 | tf_op jit(solution)/shard_map/ppermute | solution.py:290
  137.9 1.7 collective-permute-start.9
  140.3 3.8 %collective-permute-done.9 = f32[64,512]{1,0:T(8,128)S(1)} collective-permute-done((f32[64,512]{1,0:T(8,128)S(1)}, f32[64,512]{1,0:T(8,128)S(1)}, u32[]{:S(2)}, u32[]{:S(2)}) %collective-permute-start.9) | collective-permute-done | bytes 131104 | tf_op jit(solution)/shard_map/ppermute | solution.py:290
  144.1 7.0 %collective-permute-done.8 = f32[64,512]{1,0:T(8,128)S(1)} collective-permute-done((f32[64,512]{1,0:T(8,128)S(1)}, f32[64,512]{1,0:T(8,128)S(1)}, u32[]{:S(2)}, u32[]{:S(2)}) %collective-permute-start.8) | collective-permute-done | bytes 131104 | tf_op jit(solution)/shard_map/ppermute | solution.py:290
  151.2 3.4 %copy-done.1 = bf16[2,512,4096]{2,1,0:T(8,128)(2,1)S(1)} copy-done((bf16[2,512,4096]{2,1,0:T(8,128)(2,1)S(1)}, bf16[2,512,4096]{2,1,0:T(8,128)(2,1)}, u32[]{:S(2)}) %copy-start.1) | copy-done | bytes 8388632
  154.5 6.5 %shard_map.31 = (f32[4,64,256]{2,1,0:T(8,128)S(1)}, f32[4,64,256]{2,1,0:T(8,128)S(1)}) custom-call(s32[1]{0:T(128)} %bitcast.refs_0_, bf16[2,512,4096]{2,1,0:T(8,128)(2,1)S(1)} %copy-done.1, bf16[2,512,4096]{2,1,0:T(8,128)(2,1)} %refs_2_.3, bf16[256,4096]{1,0:T(8,128)(2,1)} %collective-permute-done.6.refs_3_.refs_4_, ...), custom_call_target="tpu_custom_call" | custom-call | tf_op jit(solution)/shard_map/pallas_call | solution.py:104
  161.1 1.5 collective-permute-done.10
  163.1 3.4 %collective-permute-start.13 = (f32[64,256]{1,0:T(8,128)S(1)}, f32[64,256]{1,0:T(8,128)S(1)}, u32[]{:S(2)}, u32[]{:S(2)}) collective-permute-start(f32[64,256]{1,0:T(8,128)S(1)} %get-tuple-element.66), channel_id=1, source_target_pairs={{0,6},{1,7},{2,0},{3,1},{4,2},{5,3},{6,4},{7,5},{8,14},{9,15},{10,... | collective-permute-start | bytes 196616 | tf_op jit(solution)/shard_map/ppermute | solution.py:290
  167.1 2.4 collective-permute-done.11
  169.5 3.4 %collective-permute-done.12 = f32[64,256]{1,0:T(8,128)S(1)} collective-permute-done((f32[64,256]{1,0:T(8,128)S(1)}, f32[64,256]{1,0:T(8,128)S(1)}, u32[]{:S(2)}, u32[]{:S(2)}) %collective-permute-start.12) | collective-permute-done | bytes 65568 | tf_op jit(solution)/shard_map/ppermute | solution.py:290
  173.0 2.1 collective-permute-start.16
  175.1 1.8 collective-permute-start.18
  176.9 3.2 %collective-permute-done.17 = f32[64,256]{1,0:T(8,128)S(1)} collective-permute-done((f32[64,256]{1,0:T(8,128)S(1)}, f32[64,256]{1,0:T(8,128)S(1)}, u32[]{:S(2)}, u32[]{:S(2)}) %collective-permute-start.17) | collective-permute-done | bytes 65568 | tf_op jit(solution)/shard_map/ppermute | solution.py:290
  180.8 1.5 collective-permute-done.19.refs_4_
  182.2 11.1 %collective-permute-done.14.refs_3_.refs_4_ = bf16[256,4096]{1,0:T(8,128)(2,1)} collective-permute-done((bf16[256,4096]{1,0:T(8,128)(2,1)}, bf16[256,4096]{1,0:T(8,128)(2,1)}, u32[]{:S(2)}, u32[]{:S(2)}) %collective-permute-start.14) | collective-permute-done | bytes 2097184 | tf_op jit(solution)/shard_map/ppermute | solution.py:327
  194.2 6.5 %shard_map.32 = (f32[4,64,256]{2,1,0:T(8,128)S(1)}, f32[4,64,256]{2,1,0:T(8,128)S(1)}) custom-call(s32[1]{0:T(128)} %bitcast.refs_0_, bf16[2,512,4096]{2,1,0:T(8,128)(2,1)S(1)} %copy-done.1, bf16[2,512,4096]{2,1,0:T(8,128)(2,1)} %refs_2_.3, bf16[256,4096]{1,0:T(8,128)(2,1)} %collective-permute-done.14.refs_3_.refs_4_, ...), custom_call_target="tpu_custom_call" | custom-call | tf_op jit(solution)/shard_map/pallas_call | solution.py:104
  200.8 1.5 collective-permute-done.21
  202.4 1.6 collective-permute-start.22
  204.0 2.2 collective-permute-start.24
  207.1 1.6 collective-permute-done.22
  209.3 3.4 %collective-permute-done.23 = f32[64,256]{1,0:T(8,128)S(1)} collective-permute-done((f32[64,256]{1,0:T(8,128)S(1)}, f32[64,256]{1,0:T(8,128)S(1)}, u32[]{:S(2)}, u32[]{:S(2)}) %collective-permute-start.23) | collective-permute-done | bytes 65568 | tf_op jit(solution)/shard_map/ppermute | solution.py:290
  212.7 2.3 collective-permute-start.28
  216.2 1.2 collective-permute-done.28
  217.4 4.2 %collective-permute-done.27 = f32[64,256]{1,0:T(8,128)S(1)} collective-permute-done((f32[64,256]{1,0:T(8,128)S(1)}, f32[64,256]{1,0:T(8,128)S(1)}, u32[]{:S(2)}, u32[]{:S(2)}) %collective-permute-start.27) | collective-permute-done | bytes 65568 | tf_op jit(solution)/shard_map/ppermute | solution.py:290
  222.0 1.3 collective-permute-done.29.refs_5_
  226.9 1.4 collective-permute-start.32
  228.8 1.3 collective-permute-start.33
  230.1 9.5 %collective-permute-done.32.refs_1_ = f32[2,32,512]{2,1,0:T(8,128)S(1)} collective-permute-done((f32[2,32,512]{2,1,0:T(8,128)S(1)}, f32[2,32,512]{2,1,0:T(8,128)S(1)}, u32[]{:S(2)}, u32[]{:S(2)}) %collective-permute-start.32) | collective-permute-done | bytes 131104 | tf_op jit(solution)/shard_map/ppermute | solution.py:370
  239.6 1.8 collective-permute-done.33.refs_2_
  241.4 2.5 shard_map.37
  (79 shorter events, 13.9 us)
Async XLA Ops:
  6.5 95.6 %all-reduce.3.cloned.1.call-start = ((), (), s32[]{:S(2)}) async-start(), calls=%async_computation | async-start | bytes 4194304 | tf_op jit(solution)/shard_map/psum | solution.py:334
  6.5 11.2 %copy-start = (bf16[2,512,4096]{2,1,0:T(8,128)(2,1)S(1)}, bf16[2,512,4096]{2,1,0:T(8,128)(2,1)}, u32[]{:S(2)}) copy-start(bf16[2,512,4096]{2,1,0:T(8,128)(2,1)} %refs_1_.3) | copy-start | bytes 25165828
  9.9 92.2 %collective-permute-start.1 = (bf16[256,4096]{1,0:T(8,128)(2,1)}, bf16[256,4096]{1,0:T(8,128)(2,1)S(1)}, u32[]{:S(2)}, u32[]{:S(2)}) collective-permute-start(bf16[256,4096]{1,0:T(8,128)(2,1)} %slice_bitcast_fusion), channel_id=1, source_target_pairs={{0,24},{8,0},{16,8},{24,16},{1,25},{9,1},{17,9},{25,17},{2,26},{10... | collective-permute-start | bytes 6291464 | tf_op jit(solution)/shard_map/ppermute | solution.py:327
  13.6 91.0 %collective-permute-start = (bf16[256,4096]{1,0:T(8,128)(2,1)}, bf16[256,4096]{1,0:T(8,128)(2,1)}, u32[]{:S(2)}, u32[]{:S(2)}) collective-permute-start(bf16[256,4096]{1,0:T(8,128)(2,1)} %slice_bitcast_fusion.1), channel_id=1, source_target_pairs={{0,24},{8,0},{16,8},{24,16},{1,25},{9,1},{17,9},{25,17},{2,26},{10... | collective-permute-start | bytes 6291464 | tf_op jit(solution)/shard_map/ppermute | solution.py:327
  35.6 115.5 %collective-permute-start.6 = (bf16[256,4096]{1,0:T(8,128)(2,1)}, bf16[256,4096]{1,0:T(8,128)(2,1)}, u32[]{:S(2)}, u32[]{:S(2)}) collective-permute-start(bf16[256,4096]{1,0:T(8,128)(2,1)} %pad_maximum_fusion), channel_id=1, source_target_pairs={{0,24},{8,0},{16,8},{24,16},{1,25},{9,1},{17,9},{25,17},{2,26},{10... | collective-permute-start | bytes 6291464 | tf_op jit(solution)/shard_map/ppermute | solution.py:327
  102.1 1.4 copy-start.4
  104.6 1.6 copy-start.2
  106.2 1.6 copy-start.5
  117.3 3.3 %collective-permute-start.2 = (f32[4,64,512]{2,1,0:T(8,128)S(1)}, f32[4,64,512]{2,1,0:T(8,128)}, u32[]{:S(2)}, u32[]{:S(2)}) collective-permute-start(f32[4,64,512]{2,1,0:T(8,128)S(1)} %get-tuple-element.36), channel_id=1, source_target_pairs={{0,1},{1,0},{2,3},{3,2},{4,5},{5,4},{6,7},{7,6},{8,9},{9,8},{10,11... | collective-permute-start | bytes 1572872 | tf_op jit(solution)/shard_map/ppermute | solution.py:285
  120.6 72.8 %collective-permute-start.14 = (bf16[256,4096]{1,0:T(8,128)(2,1)}, bf16[256,4096]{1,0:T(8,128)(2,1)}, u32[]{:S(2)}, u32[]{:S(2)}) collective-permute-start(bf16[256,4096]{1,0:T(8,128)(2,1)} %pad_maximum_fusion.1), channel_id=1, source_target_pairs={{0,24},{8,0},{16,8},{24,16},{1,25},{9,1},{17,9},{25,17},{2,26},{10... | collective-permute-start | bytes 6291464 | tf_op jit(solution)/shard_map/ppermute | solution.py:327
  121.7 8.2 %collective-permute-start.3 = (f32[64,512]{1,0:T(8,128)S(1)}, f32[64,512]{1,0:T(8,128)S(1)}, u32[]{:S(2)}, u32[]{:S(2)}) collective-permute-start(f32[64,512]{1,0:T(8,128)S(1)} %get-tuple-element.59), channel_id=1, source_target_pairs={{0,2},{1,3},{2,4},{3,5},{4,6},{5,7},{6,0},{7,1},{8,10},{9,11},{10,... | collective-permute-start | bytes 393224 | tf_op jit(solution)/shard_map/ppermute | solution.py:290
  123.4 8.4 %collective-permute-start.5 = (f32[64,512]{1,0:T(8,128)S(1)}, f32[64,512]{1,0:T(8,128)S(1)}, u32[]{:S(2)}, u32[]{:S(2)}) collective-permute-start(f32[64,512]{1,0:T(8,128)S(1)} %get-tuple-element.60), channel_id=1, source_target_pairs={{0,6},{1,7},{2,0},{3,1},{4,2},{5,3},{6,4},{7,5},{8,14},{9,15},{10,... | collective-permute-start | bytes 393224 | tf_op jit(solution)/shard_map/ppermute | solution.py:290
  125.6 12.3 %collective-permute-start.4 = (f32[64,512]{1,0:T(8,128)S(1)}, f32[64,512]{1,0:T(8,128)S(1)}, u32[]{:S(2)}, u32[]{:S(2)}) collective-permute-start(f32[64,512]{1,0:T(8,128)S(1)} %get-tuple-element.61), channel_id=1, source_target_pairs={{0,4},{1,5},{2,6},{3,7},{4,0},{5,1},{6,2},{7,3},{8,12},{9,13},{10,... | collective-permute-start | bytes 393224 | tf_op jit(solution)/shard_map/ppermute | solution.py:290
  137.9 6.1 %collective-permute-start.9 = (f32[64,512]{1,0:T(8,128)S(1)}, f32[64,512]{1,0:T(8,128)S(1)}, u32[]{:S(2)}, u32[]{:S(2)}) collective-permute-start(f32[64,512]{1,0:T(8,128)S(1)} %fusion.1), channel_id=1, source_target_pairs={{0,6},{1,7},{2,0},{3,1},{4,2},{5,3},{6,4},{7,5},{8,14},{9,15},{10,... | collective-permute-start | bytes 393224 | tf_op jit(solution)/shard_map/ppermute | solution.py:290
  139.6 11.5 %collective-permute-start.8 = (f32[64,512]{1,0:T(8,128)S(1)}, f32[64,512]{1,0:T(8,128)S(1)}, u32[]{:S(2)}, u32[]{:S(2)}) collective-permute-start(f32[64,512]{1,0:T(8,128)S(1)} %fusion.1), channel_id=1, source_target_pairs={{0,4},{1,5},{2,6},{3,7},{4,0},{5,1},{6,2},{7,3},{8,12},{9,13},{10,... | collective-permute-start | bytes 393224 | tf_op jit(solution)/shard_map/ppermute | solution.py:290
  139.6 11.5 %collective-permute-start.7 = (f32[64,512]{1,0:T(8,128)S(1)}, f32[64,512]{1,0:T(8,128)S(1)}, u32[]{:S(2)}, u32[]{:S(2)}) collective-permute-start(f32[64,512]{1,0:T(8,128)S(1)} %fusion.1), channel_id=1, source_target_pairs={{0,2},{1,3},{2,4},{3,5},{4,6},{5,7},{6,0},{7,1},{8,10},{9,11},{10,... | collective-permute-start | bytes 393224 | tf_op jit(solution)/shard_map/ppermute | solution.py:290
  151.1 3.4 %copy-start.1 = (bf16[2,512,4096]{2,1,0:T(8,128)(2,1)S(1)}, bf16[2,512,4096]{2,1,0:T(8,128)(2,1)}, u32[]{:S(2)}) copy-start(bf16[2,512,4096]{2,1,0:T(8,128)(2,1)} %refs_1_.3) | copy-start | bytes 25165828
  161.0 1.6 collective-permute-start.10
  162.7 6.8 %collective-permute-start.11 = (f32[64,256]{1,0:T(8,128)S(1)}, f32[64,256]{1,0:T(8,128)S(1)}, u32[]{:S(2)}, u32[]{:S(2)}) collective-permute-start(f32[64,256]{1,0:T(8,128)S(1)} %get-tuple-element.65), channel_id=1, source_target_pairs={{0,2},{1,3},{2,4},{3,5},{4,6},{5,7},{6,0},{7,1},{8,10},{9,11},{10,... | collective-permute-start | bytes 196616 | tf_op jit(solution)/shard_map/ppermute | solution.py:290
  163.1 6.3 %collective-permute-start.13 = (f32[64,256]{1,0:T(8,128)S(1)}, f32[64,256]{1,0:T(8,128)S(1)}, u32[]{:S(2)}, u32[]{:S(2)}) collective-permute-start(f32[64,256]{1,0:T(8,128)S(1)} %get-tuple-element.66), channel_id=1, source_target_pairs={{0,6},{1,7},{2,0},{3,1},{4,2},{5,3},{6,4},{7,5},{8,14},{9,15},{10,... | collective-permute-start | bytes 196616 | tf_op jit(solution)/shard_map/ppermute | solution.py:290
  166.5 6.3 %collective-permute-start.12 = (f32[64,256]{1,0:T(8,128)S(1)}, f32[64,256]{1,0:T(8,128)S(1)}, u32[]{:S(2)}, u32[]{:S(2)}) collective-permute-start(f32[64,256]{1,0:T(8,128)S(1)} %get-tuple-element.67), channel_id=1, source_target_pairs={{0,4},{1,5},{2,6},{3,7},{4,0},{5,1},{6,2},{7,3},{8,12},{9,13},{10,... | collective-permute-start | bytes 196616 | tf_op jit(solution)/shard_map/ppermute | solution.py:290
  167.1 13.7 %collective-permute-start.15 = (f32[4,64,512]{2,1,0:T(8,128)S(1)}, f32[4,64,512]{2,1,0:T(8,128)S(1)}, u32[]{:S(2)}, u32[]{:S(2)}) collective-permute-start(f32[4,64,512]{2,1,0:T(8,128)S(1)} %pad_maximum_fusion.2.refs_0_), channel_id=1, source_target_pairs={{0,1},{1,0},{2,3},{3,2},{4,5},{5,4},{6,7},{7,6},{8,9},{9,8},{10,11... | collective-permute-start | bytes 1572872 | tf_op jit(solution)/shard_map/ppermute | solution.py:285
  172.9 7.2 %collective-permute-start.17 = (f32[64,256]{1,0:T(8,128)S(1)}, f32[64,256]{1,0:T(8,128)S(1)}, u32[]{:S(2)}, u32[]{:S(2)}) collective-permute-start(f32[64,256]{1,0:T(8,128)S(1)} %fusion.7), channel_id=1, source_target_pairs={{0,4},{1,5},{2,6},{3,7},{4,0},{5,1},{6,2},{7,3},{8,12},{9,13},{10,... | collective-permute-start | bytes 196616 | tf_op jit(solution)/shard_map/ppermute | solution.py:290
  173.0 7.1 %collective-permute-start.16 = (f32[64,256]{1,0:T(8,128)S(1)}, f32[64,256]{1,0:T(8,128)S(1)}, u32[]{:S(2)}, u32[]{:S(2)}) collective-permute-start(f32[64,256]{1,0:T(8,128)S(1)} %fusion.7), channel_id=1, source_target_pairs={{0,2},{1,3},{2,4},{3,5},{4,6},{5,7},{6,0},{7,1},{8,10},{9,11},{10,... | collective-permute-start | bytes 196616 | tf_op jit(solution)/shard_map/ppermute | solution.py:290
  175.1 5.5 %collective-permute-start.18 = (f32[64,256]{1,0:T(8,128)S(1)}, f32[64,256]{1,0:T(8,128)S(1)}, u32[]{:S(2)}, u32[]{:S(2)}) collective-permute-start(f32[64,256]{1,0:T(8,128)S(1)} %fusion.7), channel_id=1, source_target_pairs={{0,6},{1,7},{2,0},{3,1},{4,2},{5,3},{6,4},{7,5},{8,14},{9,15},{10,... | collective-permute-start | bytes 196616 | tf_op jit(solution)/shard_map/ppermute | solution.py:290
  180.6 1.6 collective-permute-start.19
  182.2 18.4 %copy-start.6 = (f32[4,64,256]{2,1,0:T(8,128)}, f32[4,64,256]{2,1,0:T(8,128)S(1)}, u32[]{:S(2)}) copy-start(f32[4,64,256]{2,1,0:T(8,128)S(1)} %collective-permute-done.19.refs_4_) | copy-start | bytes 786436
  193.3 7.4 %collective-permute-start.20 = (f32[64,768]{1,0:T(8,128)S(1)}, f32[64,768]{1,0:T(8,128)S(1)}, u32[]{:S(2)}, u32[]{:S(2)}) collective-permute-start(f32[64,768]{1,0:T(8,128)S(1)} %pad_maximum_fusion.6), channel_id=1, source_target_pairs={{0,8},{1,9},{2,10},{3,11},{4,12},{5,13},{6,14},{7,15}} | collective-permute-start | bytes 589832 | tf_op jit(solution)/shard_map/ppermute | solution.py:348
  200.7 1.7 copy-start.8
  200.7 22.6 %copy-start.7 = (f32[4,64,256]{2,1,0:T(8,128)S(1)}, f32[4,64,256]{2,1,0:T(8,128)}, u32[]{:S(2)}) copy-start(f32[4,64,256]{2,1,0:T(8,128)} %copy-done.6) | copy-start | bytes 786436
  200.7 1.6 collective-permute-start.21
  202.4 6.2 %collective-permute-start.22 = (f32[64,256]{1,0:T(8,128)S(1)}, f32[64,256]{1,0:T(8,128)S(1)}, u32[]{:S(2)}, u32[]{:S(2)}) collective-permute-start(f32[64,256]{1,0:T(8,128)S(1)} %get-tuple-element.62), channel_id=1, source_target_pairs={{0,2},{1,3},{2,4},{3,5},{4,6},{5,7},{6,0},{7,1},{8,10},{9,11},{10,... | collective-permute-start | bytes 196616 | tf_op jit(solution)/shard_map/ppermute | solution.py:290
  204.0 5.3 %collective-permute-start.24 = (f32[64,256]{1,0:T(8,128)S(1)}, f32[64,256]{1,0:T(8,128)S(1)}, u32[]{:S(2)}, u32[]{:S(2)}) collective-permute-start(f32[64,256]{1,0:T(8,128)S(1)} %get-tuple-element.63), channel_id=1, source_target_pairs={{0,6},{1,7},{2,0},{3,1},{4,2},{5,3},{6,4},{7,5},{8,14},{9,15},{10,... | collective-permute-start | bytes 196616 | tf_op jit(solution)/shard_map/ppermute | solution.py:290
  206.3 6.4 %collective-permute-start.23 = (f32[64,256]{1,0:T(8,128)S(1)}, f32[64,256]{1,0:T(8,128)S(1)}, u32[]{:S(2)}, u32[]{:S(2)}) collective-permute-start(f32[64,256]{1,0:T(8,128)S(1)} %get-tuple-element.64), channel_id=1, source_target_pairs={{0,4},{1,5},{2,6},{3,7},{4,0},{5,1},{6,2},{7,3},{8,12},{9,13},{10,... | collective-permute-start | bytes 196616 | tf_op jit(solution)/shard_map/ppermute | solution.py:290
  212.7 4.8 %collective-permute-start.28 = (f32[64,256]{1,0:T(8,128)S(1)}, f32[64,256]{1,0:T(8,128)S(1)}, u32[]{:S(2)}, u32[]{:S(2)}) collective-permute-start(f32[64,256]{1,0:T(8,128)S(1)} %fusion.5), channel_id=1, source_target_pairs={{0,6},{1,7},{2,0},{3,1},{4,2},{5,3},{6,4},{7,5},{8,14},{9,15},{10,... | collective-permute-start | bytes 196616 | tf_op jit(solution)/shard_map/ppermute | solution.py:290
  214.9 6.7 %collective-permute-start.27 = (f32[64,256]{1,0:T(8,128)S(1)}, f32[64,256]{1,0:T(8,128)S(1)}, u32[]{:S(2)}, u32[]{:S(2)}) collective-permute-start(f32[64,256]{1,0:T(8,128)S(1)} %fusion.5), channel_id=1, source_target_pairs={{0,4},{1,5},{2,6},{3,7},{4,0},{5,1},{6,2},{7,3},{8,12},{9,13},{10,... | collective-permute-start | bytes 196616 | tf_op jit(solution)/shard_map/ppermute | solution.py:290
  214.9 6.7 %collective-permute-start.26 = (f32[64,256]{1,0:T(8,128)S(1)}, f32[64,256]{1,0:T(8,128)S(1)}, u32[]{:S(2)}, u32[]{:S(2)}) collective-permute-start(f32[64,256]{1,0:T(8,128)S(1)} %fusion.5), channel_id=1, source_target_pairs={{0,2},{1,3},{2,4},{3,5},{4,6},{5,7},{6,0},{7,1},{8,10},{9,11},{10,... | collective-permute-start | bytes 196616 | tf_op jit(solution)/shard_map/ppermute | solution.py:290
  215.6 6.1 %collective-permute-start.25 = (f32[64,256]{1,0:T(8,128)S(1)}, f32[64,256]{1,0:T(8,128)S(1)}, u32[]{:S(2)}, u32[]{:S(2)}) collective-permute-start(f32[64,256]{1,0:T(8,128)S(1)} %fusion.5), channel_id=1, source_target_pairs={{0,8},{1,9},{2,10},{3,11},{4,12},{5,13},{6,14},{7,15}} | collective-permute-start | bytes 196616 | tf_op jit(solution)/shard_map/ppermute | solution.py:357
  221.7 1.6 collective-permute-start.29
  222.0 2.3 copy-start.9
  225.0 1.4 collective-permute-start.30
  225.7 2.6 %collective-permute-start.31 = (f32[2,32,512]{2,1,0:T(8,128)S(1)}, f32[2,32,512]{2,1,0:T(8,128)S(1)}, u32[]{:S(2)}, u32[]{:S(2)}) collective-permute-start(f32[2,32,512]{2,1,0:T(8,128)S(1)} %get-tuple-element.51), channel_id=1, source_target_pairs={{8,16},{9,17},{10,18},{11,19},{12,20},{13,21},{14,22},{15,23}} | collective-permute-start | bytes 393224 | tf_op jit(solution)/shard_map/ppermute | solution.py:370
  226.8 14.6 %copy-start.3 = (f32[512,1024]{1,0:T(8,128)S(1)}, f32[512,1024]{1,0:T(8,128)}, u32[]{:S(2)}) copy-start(f32[512,1024]{1,0:T(8,128)} %all-reduce.3.cloned.1.call-done.value.refs_3_) | copy-start | bytes 6291460
  226.9 12.8 %collective-permute-start.32 = (f32[2,32,512]{2,1,0:T(8,128)S(1)}, f32[2,32,512]{2,1,0:T(8,128)S(1)}, u32[]{:S(2)}, u32[]{:S(2)}) collective-permute-start(f32[2,32,512]{2,1,0:T(8,128)S(1)} %get-tuple-element.53), channel_id=1, source_target_pairs={{16,24},{17,25},{18,26},{19,27},{20,28},{21,29},{22,30},{23,31}} | collective-permute-start | bytes 393224 | tf_op jit(solution)/shard_map/ppermute | solution.py:370
  228.8 12.7 %collective-permute-start.33 = (f32[2,32,512]{2,1,0:T(8,128)S(1)}, f32[2,32,512]{2,1,0:T(8,128)S(1)}, u32[]{:S(2)}, u32[]{:S(2)}) collective-permute-start(f32[2,32,512]{2,1,0:T(8,128)S(1)} %get-tuple-element.54), channel_id=1, source_target_pairs={{16,24},{17,25},{18,26},{19,27},{20,28},{21,29},{22,30},{23,31}} | collective-permute-start | bytes 393224 | tf_op jit(solution)/shard_map/ppermute | solution.py:370
Sparse Core Ops, SparseCore 0:
  35.8 66.3 all-reduce.2
where the time goes:
time: 252 us; the launch traced here: 251 us
  waiting for transfers between devices  138 us (55%)
  Pallas kernels  41.4 us (16%)
  starting transfers between devices  31.3 us (12%)
  local copies, waits for them, and re-layouts  19.8 us (8%)
  between operations  13.9 us (6%)
  other arithmetic  6.21 us (2%)
    psum x1, waiting for transfers between devices, shards(): own_margins = [lax.psum(term, 'pw') for term in terms]  66 us
    ppermute x18, waiting for transfers between devices, other_chip(): lax.ppermute(block, 'pw', [(i, (i + 2 * distance) % size) for i in range(...  42.9 us
    pallas_call x4, Pallas kernels, margin_section(): pl.pallas_call(functools.partial(margin_kernel, steps, len(other_specs) /...  36 us
    ppermute x18, starting transfers between devices, other_chip(): lax.ppermute(block, 'pw', [(i, (i + 2 * distance) % size) for i in range(...  22.9 us
    ppermute x4, waiting for transfers between devices, send(): lax.ppermute(after(blocks[number], earlier) if earlier else blocks[number...  12.1 us
    ppermute x4, waiting for transfers between devices, shards(): lax.ppermute(line, 'ka', [(number, number + 1)])  11.3 us
    unnamed x20, local copies, waits for them, and re-layouts  7.7 us
    squeeze x2, local copies, waits for them, and re-layouts, shards(): blocks = [tuple((state[0, :widths[0]] for state in (states_re, states_im)))]  6.5 us
  transfers between devices with their start and end apart: 35, of which 23 were waited for; matrix products, arithmetic and copies ran while one was open for 6% of the time, Pallas kernels for 15%

commit v1 on v0

--- a/solution.py
+++ b/solution.py
@@ -244,13 +244,14 @@
 def last_kernel(widths, parts, *refs):
     before, *refs = refs
     received, (*margins, span, out) = refs[:parts], refs[parts:]
+    margins = [halves_of(margin[...]) for margin in margins]
     for part, ref in enumerate(received):
         count = ref.shape[1]
         where = slice(part * count, (part + 1) * count)
         reals, imags = before[0, where, :] + ref[0], before[1, where, :] + ref[1]
         both, high = split_rows(jnp.concatenate([reals, imags], 0))
         for i, margin in enumerate(margins):
-            times_into(out.at[i, where], True, both, high, [halves_of(margin[...])])
+            times_into(out.at[i, where], True, both, high, [margin])
         times_into(out.at[len(margins), where], True, both, high, span_pieces(span, widths))
 
 
@@ -345,7 +346,7 @@
         if final:
             reals = [one[:, : one.shape[1] // 2] for one in rows]
             imags = [one[:, one.shape[1] // 2 :] for one in rows]
-            ready = lax.ppermute(after(jnp.concatenate(reals + imags, 1), (piece, swapped)), "ka", [(0, 1)])
+            ready = lax.ppermute(after(jnp.concatenate(reals + imags, 1), swapped), "ka", [(0, 1)])
         if halves:
             piece = after(piece, halves[-1])
         mine, theirs = margin_section(states, last, [piece], left, core)

time: 252 us -> 250 us (level)
    unnamed x20 -> x24, local copies, waits for them, and re-layouts: 7.7 us -> 7.71 us
  transfers between devices with their start and end apart: 35 -> 35, of which waited for: 23 -> 25; matrix products, arithmetic and copies ran while one was open for 6% -> 5% of each run, Pallas kernels for 15% -> 15%
where the time goes in v1:
time: 250 us
  waiting for transfers between devices  139 us (56%)
  Pallas kernels  41.3 us (17%)
  starting transfers between devices  31.6 us (13%)
  local copies, waits for them, and re-layouts  19.8 us (8%)
  between operations  13.8 us (6%)
  other arithmetic  4.67 us (2%)
    psum x1, waiting for transfers between devices, shards(): own_margins = [lax.psum(term, 'pw') for term in terms]  66 us
    ppermute x18, waiting for transfers between devices, other_chip(): lax.ppermute(block, 'pw', [(i, (i + 2 * distance) % size) for i in range(...  41.8 us
    pallas_call x4, Pallas kernels, margin_section(): pl.pallas_call(functools.partial(margin_kernel, steps, len(other_specs) /...  36 us
    ppermute x18, starting transfers between devices, other_chip(): lax.ppermute(block, 'pw', [(i, (i + 2 * distance) % size) for i in range(...  23.1 us
    ppermute x4, waiting for transfers between devices, send(): lax.ppermute(after(blocks[number], earlier) if earlier else blocks[number...  12.8 us
    ppermute x4, waiting for transfers between devices, shards(): lax.ppermute(line, 'ka', [(number, number + 1)])  10.2 us
    unnamed x24, local copies, waits for them, and re-layouts  7.71 us
    ppermute x6, waiting for transfers between devices, other_core(): return lax.ppermute(block, 'pw', [(i, i ^ 1) for i in range(size)])  7.68 us
  transfers between devices with their start and end apart: 35, of which 25 were waited for; matrix products, arithmetic and copies ran while one was open for 5% of the time, Pallas kernels for 15%

profile of v1, /device:TPU:6, one launch (start us, length us, event | category | flops | bytes accessed | tf_op | source)
XLA Modules:
  0.0 249.8 jit_solution(8409261928471192178)
XLA Ops:
  6.5 3.4 %slice_bitcast_fusion = bf16[256,4096]{1,0:T(8,128)(2,1)} fusion(bf16[2,512,4096]{2,1,0:T(8,128)(2,1)} %refs_2_.3), kind=kLoop, calls=%fused_computation.2 | loop fusion | bytes 4194304 | tf_op jit(solution)/shard_map/squeeze | solution.py:324
  10.5 3.1 %slice_bitcast_fusion.1 = bf16[256,4096]{1,0:T(8,128)(2,1)} fusion(bf16[2,512,4096]{2,1,0:T(8,128)(2,1)} %refs_1_.3), kind=kLoop, calls=%fused_computation.3 | loop fusion | bytes 4194304 | tf_op jit(solution)/shard_map/squeeze | solution.py:324
  13.6 1.4 collective-permute-start
  15.0 2.7 %slice_bitcast_fusion.3 = (bf16[128,4096]{1,0:T(8,128)(2,1)}, bf16[128,4096]{1,0:T(8,128)(2,1)S(1)}) fusion(bf16[2,512,4096]{2,1,0:T(8,128)(2,1)} %refs_1_.3), kind=kLoop, calls=%fused_computation.5 | loop fusion | bytes 4194304 | tf_op jit(solution)/shard_map/squeeze | solution.py:277
  17.7 13.6 %shard_map.28 = f32[512,1024]{1,0:T(8,128)} custom-call(bf16[2,512,4096]{2,1,0:T(8,128)(2,1)S(1)} %copy-done, bf16[2,512,4096]{2,1,0:T(8,128)(2,1)} %refs_2_.3, bf16[2,512,4096]{2,1,0:T(8,128)(2,1)S(1)} %copy-done, bf16[2,512,4096]{2,1,0:T(8,128)(2,1)} %refs_2_.3), custom_call_target="tpu_custom_call" | custom-call | tf_op jit(solution)/shard_map/pallas_call | solution.py:104
  31.3 2.7 %slice_bitcast_fusion.2 = (bf16[128,4096]{1,0:T(8,128)(2,1)}, bf16[128,4096]{1,0:T(8,128)(2,1)S(1)}) fusion(bf16[2,512,4096]{2,1,0:T(8,128)(2,1)} %refs_2_.3), kind=kLoop, calls=%fused_computation.4 | loop fusion | bytes 4194304 | tf_op jit(solution)/shard_map/squeeze | solution.py:277
  34.1 1.6 pad_maximum_fusion
  36.1 66.0 %all-reduce.3.cloned.1.call-done.value.refs_3_ = f32[512,1024]{1,0:T(8,128)} async-done(((f32[512,1024]{1,0:T(8,128)}), f32[512,1024]{1,0:T(8,128)}) %all-reduce.3.cloned.1.call-update) | async-done | bytes 2097168 | tf_op jit(solution)/shard_map/psum | solution.py:335
  102.1 1.4 copy-done.4
  104.6 1.6 copy-done.2
  106.5 1.3 copy-done.5
  107.8 9.5 %shard_map.30 = (f32[4,64,512]{2,1,0:T(8,128)S(1)}, f32[4,64,512]{2,1,0:T(8,128)S(1)}) custom-call(s32[1]{0:T(128)} %bitcast.refs_0_, bf16[2,512,4096]{2,1,0:T(8,128)(2,1)} %refs_1_.3, bf16[2,512,4096]{2,1,0:T(8,128)(2,1)} %refs_2_.3, bf16[256,4096]{1,0:T(8,128)(2,1)} %collective-permute-done.refs_3_, bf16[256,4096]{1,0:T(8,128)(2,1)S(1)} %copy-done.5, ...), custom_call_target="tpu_custom_call" | custom-call | tf_op jit(solution)/shard_map/pallas_call | solution.py:104
  117.4 1.9 collective-permute-done.2
  120.5 1.6 collective-permute-start.3
  122.2 2.2 collective-permute-start.5
  125.2 1.6 pad_maximum_fusion.1
  126.8 1.9 collective-permute-done.3
  128.8 1.5 collective-permute-done.5
  130.2 6.2 %collective-permute-done.4 = f32[64,512]{1,0:T(8,128)S(1)} collective-permute-done((f32[64,512]{1,0:T(8,128)S(1)}, f32[64,512]{1,0:T(8,128)S(1)}, u32[]{:S(2)}, u32[]{:S(2)}) %collective-permute-start.4) | collective-permute-done | bytes 131104 | tf_op jit(solution)/shard_map/ppermute | solution.py:291
  136.5 1.7 collective-permute-start.9
  138.8 3.8 %collective-permute-done.9 = f32[64,512]{1,0:T(8,128)S(1)} collective-permute-done((f32[64,512]{1,0:T(8,128)S(1)}, f32[64,512]{1,0:T(8,128)S(1)}, u32[]{:S(2)}, u32[]{:S(2)}) %collective-permute-start.9) | collective-permute-done | bytes 131104 | tf_op jit(solution)/shard_map/ppermute | solution.py:291
  142.6 6.9 %collective-permute-done.8 = f32[64,512]{1,0:T(8,128)S(1)} collective-permute-done((f32[64,512]{1,0:T(8,128)S(1)}, f32[64,512]{1,0:T(8,128)S(1)}, u32[]{:S(2)}, u32[]{:S(2)}) %collective-permute-start.8) | collective-permute-done | bytes 131104 | tf_op jit(solution)/shard_map/ppermute | solution.py:291
  149.6 3.4 %copy-done.1 = bf16[2,512,4096]{2,1,0:T(8,128)(2,1)S(1)} copy-done((bf16[2,512,4096]{2,1,0:T(8,128)(2,1)S(1)}, bf16[2,512,4096]{2,1,0:T(8,128)(2,1)}, u32[]{:S(2)}) %copy-start.1) | copy-done | bytes 8388632
  152.9 6.5 %shard_map.31 = (f32[4,64,256]{2,1,0:T(8,128)S(1)}, f32[4,64,256]{2,1,0:T(8,128)S(1)}) custom-call(s32[1]{0:T(128)} %bitcast.refs_0_, bf16[2,512,4096]{2,1,0:T(8,128)(2,1)S(1)} %copy-done.1, bf16[2,512,4096]{2,1,0:T(8,128)(2,1)} %refs_2_.3, bf16[256,4096]{1,0:T(8,128)(2,1)} %collective-permute-done.6.refs_3_.refs_4_, ...), custom_call_target="tpu_custom_call" | custom-call | tf_op jit(solution)/shard_map/pallas_call | solution.py:104
  159.5 1.5 collective-permute-done.10
  161.1 1.6 collective-permute-start.11
  162.7 2.3 collective-permute-start.13
  165.7 1.6 collective-permute-done.11
  167.9 3.4 %collective-permute-done.12 = f32[64,256]{1,0:T(8,128)S(1)} collective-permute-done((f32[64,256]{1,0:T(8,128)S(1)}, f32[64,256]{1,0:T(8,128)S(1)}, u32[]{:S(2)}, u32[]{:S(2)}) %collective-permute-start.12) | collective-permute-done | bytes 65568 | tf_op jit(solution)/shard_map/ppermute | solution.py:291
  171.4 2.8 %collective-permute-start.15 = (f32[64,256]{1,0:T(8,128)S(1)}, f32[64,256]{1,0:T(8,128)S(1)}, u32[]{:S(2)}, u32[]{:S(2)}) collective-permute-start(f32[64,256]{1,0:T(8,128)S(1)} %fusion.7), channel_id=1, source_target_pairs={{0,2},{1,3},{2,4},{3,5},{4,6},{5,7},{6,0},{7,1},{8,10},{9,11},{10,... | collective-permute-start | bytes 196616 | tf_op jit(solution)/shard_map/ppermute | solution.py:291
  175.3 3.6 %collective-permute-done.16 = f32[64,256]{1,0:T(8,128)S(1)} collective-permute-done((f32[64,256]{1,0:T(8,128)S(1)}, f32[64,256]{1,0:T(8,128)S(1)}, u32[]{:S(2)}, u32[]{:S(2)}) %collective-permute-start.16) | collective-permute-done | bytes 65568 | tf_op jit(solution)/shard_map/ppermute | solution.py:291
  178.9 1.3 collective-permute-done.17
  180.4 1.4 collective-permute-done.18.refs_4_
  182.7 11.8 %collective-permute-done.20.refs_3_.refs_4_ = bf16[256,4096]{1,0:T(8,128)(2,1)} collective-permute-done((bf16[256,4096]{1,0:T(8,128)(2,1)}, bf16[256,4096]{1,0:T(8,128)(2,1)}, u32[]{:S(2)}, u32[]{:S(2)}) %collective-permute-start.20) | collective-permute-done | bytes 2097184 | tf_op jit(solution)/shard_map/ppermute | solution.py:328
  194.5 6.5 %shard_map.32 = (f32[4,64,256]{2,1,0:T(8,128)S(1)}, f32[4,64,256]{2,1,0:T(8,128)S(1)}) custom-call(s32[1]{0:T(128)} %bitcast.refs_0_, bf16[2,512,4096]{2,1,0:T(8,128)(2,1)S(1)} %copy-done.1, bf16[2,512,4096]{2,1,0:T(8,128)(2,1)} %refs_2_.3, bf16[256,4096]{1,0:T(8,128)(2,1)} %collective-permute-done.20.refs_3_.refs_4_, ...), custom_call_target="tpu_custom_call" | custom-call | tf_op jit(solution)/shard_map/pallas_call | solution.py:104
  201.1 1.5 collective-permute-done.21
  202.7 1.6 collective-permute-start.22
  204.3 2.3 collective-permute-start.24
  207.3 1.6 collective-permute-done.22
  209.6 3.4 %collective-permute-done.23 = f32[64,256]{1,0:T(8,128)S(1)} collective-permute-done((f32[64,256]{1,0:T(8,128)S(1)}, f32[64,256]{1,0:T(8,128)S(1)}, u32[]{:S(2)}, u32[]{:S(2)}) %collective-permute-start.23) | collective-permute-done | bytes 65568 | tf_op jit(solution)/shard_map/ppermute | solution.py:291
  212.9 2.3 collective-permute-start.28
  217.7 4.2 %collective-permute-done.27 = f32[64,256]{1,0:T(8,128)S(1)} collective-permute-done((f32[64,256]{1,0:T(8,128)S(1)}, f32[64,256]{1,0:T(8,128)S(1)}, u32[]{:S(2)}, u32[]{:S(2)}) %collective-permute-start.27) | collective-permute-done | bytes 65568 | tf_op jit(solution)/shard_map/ppermute | solution.py:291
  222.3 1.3 collective-permute-done.29.refs_5_
  227.2 1.4 collective-permute-start.32
  229.1 1.3 collective-permute-start.33
  230.4 8.4 %collective-permute-done.32.refs_1_ = f32[2,32,512]{2,1,0:T(8,128)S(1)} collective-permute-done((f32[2,32,512]{2,1,0:T(8,128)S(1)}, f32[2,32,512]{2,1,0:T(8,128)S(1)}, u32[]{:S(2)}, u32[]{:S(2)}) %collective-permute-start.32) | collective-permute-done | bytes 131104 | tf_op jit(solution)/shard_map/ppermute | solution.py:371
  238.7 1.8 collective-permute-done.33.refs_2_
  240.6 2.4 shard_map.37
  (83 shorter events, 17.3 us)
Async XLA Ops:
  6.5 95.6 %all-reduce.3.cloned.1.call-start = ((), (), s32[]{:S(2)}) async-start(), calls=%async_computation | async-start | bytes 4194304 | tf_op jit(solution)/shard_map/psum | solution.py:335
  6.5 11.2 %copy-start = (bf16[2,512,4096]{2,1,0:T(8,128)(2,1)S(1)}, bf16[2,512,4096]{2,1,0:T(8,128)(2,1)}, u32[]{:S(2)}) copy-start(bf16[2,512,4096]{2,1,0:T(8,128)(2,1)} %refs_1_.3) | copy-start | bytes 25165828
  9.9 92.2 %collective-permute-start.1 = (bf16[256,4096]{1,0:T(8,128)(2,1)}, bf16[256,4096]{1,0:T(8,128)(2,1)S(1)}, u32[]{:S(2)}, u32[]{:S(2)}) collective-permute-start(bf16[256,4096]{1,0:T(8,128)(2,1)} %slice_bitcast_fusion), channel_id=1, source_target_pairs={{0,24},{8,0},{16,8},{24,16},{1,25},{9,1},{17,9},{25,17},{2,26},{10... | collective-permute-start | bytes 6291464 | tf_op jit(solution)/shard_map/ppermute | solution.py:328
  13.6 91.0 %collective-permute-start = (bf16[256,4096]{1,0:T(8,128)(2,1)}, bf16[256,4096]{1,0:T(8,128)(2,1)}, u32[]{:S(2)}, u32[]{:S(2)}) collective-permute-start(bf16[256,4096]{1,0:T(8,128)(2,1)} %slice_bitcast_fusion.1), channel_id=1, source_target_pairs={{0,24},{8,0},{16,8},{24,16},{1,25},{9,1},{17,9},{25,17},{2,26},{10... | collective-permute-start | bytes 6291464 | tf_op jit(solution)/shard_map/ppermute | solution.py:328
  35.6 113.9 %collective-permute-start.6 = (bf16[256,4096]{1,0:T(8,128)(2,1)}, bf16[256,4096]{1,0:T(8,128)(2,1)}, u32[]{:S(2)}, u32[]{:S(2)}) collective-permute-start(bf16[256,4096]{1,0:T(8,128)(2,1)} %pad_maximum_fusion), channel_id=1, source_target_pairs={{0,24},{8,0},{16,8},{24,16},{1,25},{9,1},{17,9},{25,17},{2,26},{10... | collective-permute-start | bytes 6291464 | tf_op jit(solution)/shard_map/ppermute | solution.py:328
  102.1 1.4 copy-start.4
  104.6 1.6 copy-start.2
  106.2 1.6 copy-start.5
  117.3 2.1 collective-permute-start.2
  117.4 7.8 %copy-start.10 = (bf16[128,4096]{1,0:T(8,128)(2,1)S(1)}, bf16[128,4096]{1,0:T(8,128)(2,1)}, u32[]{:S(2)}) copy-start(bf16[128,4096]{1,0:T(8,128)(2,1)} %get-tuple-element.55) | copy-start | bytes 3145732
  117.4 7.8 %copy-start.11 = (bf16[128,4096]{1,0:T(8,128)(2,1)S(1)}, bf16[128,4096]{1,0:T(8,128)(2,1)}, u32[]{:S(2)}) copy-start(bf16[128,4096]{1,0:T(8,128)(2,1)} %get-tuple-element.57) | copy-start | bytes 3145732
  120.5 8.2 %collective-permute-start.3 = (f32[64,512]{1,0:T(8,128)S(1)}, f32[64,512]{1,0:T(8,128)S(1)}, u32[]{:S(2)}, u32[]{:S(2)}) collective-permute-start(f32[64,512]{1,0:T(8,128)S(1)} %get-tuple-element.59), channel_id=1, source_target_pairs={{0,2},{1,3},{2,4},{3,5},{4,6},{5,7},{6,0},{7,1},{8,10},{9,11},{10,... | collective-permute-start | bytes 393224 | tf_op jit(solution)/shard_map/ppermute | solution.py:291
  122.2 8.1 %collective-permute-start.5 = (f32[64,512]{1,0:T(8,128)S(1)}, f32[64,512]{1,0:T(8,128)S(1)}, u32[]{:S(2)}, u32[]{:S(2)}) collective-permute-start(f32[64,512]{1,0:T(8,128)S(1)} %get-tuple-element.60), channel_id=1, source_target_pairs={{0,6},{1,7},{2,0},{3,1},{4,2},{5,3},{6,4},{7,5},{8,14},{9,15},{10,... | collective-permute-start | bytes 393224 | tf_op jit(solution)/shard_map/ppermute | solution.py:291
  124.4 12.0 %collective-permute-start.4 = (f32[64,512]{1,0:T(8,128)S(1)}, f32[64,512]{1,0:T(8,128)S(1)}, u32[]{:S(2)}, u32[]{:S(2)}) collective-permute-start(f32[64,512]{1,0:T(8,128)S(1)} %get-tuple-element.61), channel_id=1, source_target_pairs={{0,4},{1,5},{2,6},{3,7},{4,0},{5,1},{6,2},{7,3},{8,12},{9,13},{10,... | collective-permute-start | bytes 393224 | tf_op jit(solution)/shard_map/ppermute | solution.py:291
  126.8 67.7 %collective-permute-start.20 = (bf16[256,4096]{1,0:T(8,128)(2,1)}, bf16[256,4096]{1,0:T(8,128)(2,1)}, u32[]{:S(2)}, u32[]{:S(2)}) collective-permute-start(bf16[256,4096]{1,0:T(8,128)(2,1)} %pad_maximum_fusion.1), channel_id=1, source_target_pairs={{0,24},{8,0},{16,8},{24,16},{1,25},{9,1},{17,9},{25,17},{2,26},{10... | collective-permute-start | bytes 6291464 | tf_op jit(solution)/shard_map/ppermute | solution.py:328
  136.5 6.1 %collective-permute-start.9 = (f32[64,512]{1,0:T(8,128)S(1)}, f32[64,512]{1,0:T(8,128)S(1)}, u32[]{:S(2)}, u32[]{:S(2)}) collective-permute-start(f32[64,512]{1,0:T(8,128)S(1)} %fusion.1), channel_id=1, source_target_pairs={{0,6},{1,7},{2,0},{3,1},{4,2},{5,3},{6,4},{7,5},{8,14},{9,15},{10,... | collective-permute-start | bytes 393224 | tf_op jit(solution)/shard_map/ppermute | solution.py:291
  138.2 11.4 %collective-permute-start.8 = (f32[64,512]{1,0:T(8,128)S(1)}, f32[64,512]{1,0:T(8,128)S(1)}, u32[]{:S(2)}, u32[]{:S(2)}) collective-permute-start(f32[64,512]{1,0:T(8,128)S(1)} %fusion.1), channel_id=1, source_target_pairs={{0,4},{1,5},{2,6},{3,7},{4,0},{5,1},{6,2},{7,3},{8,12},{9,13},{10,... | collective-permute-start | bytes 393224 | tf_op jit(solution)/shard_map/ppermute | solution.py:291
  138.2 11.4 %collective-permute-start.7 = (f32[64,512]{1,0:T(8,128)S(1)}, f32[64,512]{1,0:T(8,128)S(1)}, u32[]{:S(2)}, u32[]{:S(2)}) collective-permute-start(f32[64,512]{1,0:T(8,128)S(1)} %fusion.1), channel_id=1, source_target_pairs={{0,2},{1,3},{2,4},{3,5},{4,6},{5,7},{6,0},{7,1},{8,10},{9,11},{10,... | collective-permute-start | bytes 393224 | tf_op jit(solution)/shard_map/ppermute | solution.py:291
  149.6 3.4 %copy-start.1 = (bf16[2,512,4096]{2,1,0:T(8,128)(2,1)S(1)}, bf16[2,512,4096]{2,1,0:T(8,128)(2,1)}, u32[]{:S(2)}) copy-start(bf16[2,512,4096]{2,1,0:T(8,128)(2,1)} %refs_1_.3) | copy-start | bytes 25165828
  159.4 1.6 collective-permute-start.10
  161.1 6.2 %collective-permute-start.11 = (f32[64,256]{1,0:T(8,128)S(1)}, f32[64,256]{1,0:T(8,128)S(1)}, u32[]{:S(2)}, u32[]{:S(2)}) collective-permute-start(f32[64,256]{1,0:T(8,128)S(1)} %get-tuple-element.65), channel_id=1, source_target_pairs={{0,2},{1,3},{2,4},{3,5},{4,6},{5,7},{6,0},{7,1},{8,10},{9,11},{10,... | collective-permute-start | bytes 196616 | tf_op jit(solution)/shard_map/ppermute | solution.py:291
  162.7 5.3 %collective-permute-start.13 = (f32[64,256]{1,0:T(8,128)S(1)}, f32[64,256]{1,0:T(8,128)S(1)}, u32[]{:S(2)}, u32[]{:S(2)}) collective-permute-start(f32[64,256]{1,0:T(8,128)S(1)} %get-tuple-element.66), channel_id=1, source_target_pairs={{0,6},{1,7},{2,0},{3,1},{4,2},{5,3},{6,4},{7,5},{8,14},{9,15},{10,... | collective-permute-start | bytes 196616 | tf_op jit(solution)/shard_map/ppermute | solution.py:291
  165.0 6.4 %collective-permute-start.12 = (f32[64,256]{1,0:T(8,128)S(1)}, f32[64,256]{1,0:T(8,128)S(1)}, u32[]{:S(2)}, u32[]{:S(2)}) collective-permute-start(f32[64,256]{1,0:T(8,128)S(1)} %get-tuple-element.67), channel_id=1, source_target_pairs={{0,4},{1,5},{2,6},{3,7},{4,0},{5,1},{6,2},{7,3},{8,12},{9,13},{10,... | collective-permute-start | bytes 196616 | tf_op jit(solution)/shard_map/ppermute | solution.py:291
  165.7 14.7 %collective-permute-start.14 = (f32[4,64,512]{2,1,0:T(8,128)S(1)}, f32[4,64,512]{2,1,0:T(8,128)S(1)}, u32[]{:S(2)}, u32[]{:S(2)}) collective-permute-start(f32[4,64,512]{2,1,0:T(8,128)S(1)} %pad_maximum_fusion.2.refs_0_), channel_id=1, source_target_pairs={{0,1},{1,0},{2,3},{3,2},{4,5},{5,4},{6,7},{7,6},{8,9},{9,8},{10,11... | collective-permute-start | bytes 1572872 | tf_op jit(solution)/shard_map/ppermute | solution.py:286
  171.3 7.6 %collective-permute-start.16 = (f32[64,256]{1,0:T(8,128)S(1)}, f32[64,256]{1,0:T(8,128)S(1)}, u32[]{:S(2)}, u32[]{:S(2)}) collective-permute-start(f32[64,256]{1,0:T(8,128)S(1)} %fusion.7), channel_id=1, source_target_pairs={{0,4},{1,5},{2,6},{3,7},{4,0},{5,1},{6,2},{7,3},{8,12},{9,13},{10,... | collective-permute-start | bytes 196616 | tf_op jit(solution)/shard_map/ppermute | solution.py:291
  171.4 7.5 %collective-permute-start.15 = (f32[64,256]{1,0:T(8,128)S(1)}, f32[64,256]{1,0:T(8,128)S(1)}, u32[]{:S(2)}, u32[]{:S(2)}) collective-permute-start(f32[64,256]{1,0:T(8,128)S(1)} %fusion.7), channel_id=1, source_target_pairs={{0,2},{1,3},{2,4},{3,5},{4,6},{5,7},{6,0},{7,1},{8,10},{9,11},{10,... | collective-permute-start | bytes 196616 | tf_op jit(solution)/shard_map/ppermute | solution.py:291
  174.2 6.0 %collective-permute-start.17 = (f32[64,256]{1,0:T(8,128)S(1)}, f32[64,256]{1,0:T(8,128)S(1)}, u32[]{:S(2)}, u32[]{:S(2)}) collective-permute-start(f32[64,256]{1,0:T(8,128)S(1)} %fusion.7), channel_id=1, source_target_pairs={{0,6},{1,7},{2,0},{3,1},{4,2},{5,3},{6,4},{7,5},{8,14},{9,15},{10,... | collective-permute-start | bytes 196616 | tf_op jit(solution)/shard_map/ppermute | solution.py:291
  180.2 1.6 collective-permute-start.18
  181.8 19.1 %copy-start.6 = (f32[4,64,256]{2,1,0:T(8,128)}, f32[4,64,256]{2,1,0:T(8,128)S(1)}, u32[]{:S(2)}) copy-start(f32[4,64,256]{2,1,0:T(8,128)S(1)} %collective-permute-done.18.refs_4_) | copy-start | bytes 786436
  181.8 19.1 %collective-permute-start.19 = (f32[64,768]{1,0:T(8,128)S(1)}, f32[64,768]{1,0:T(8,128)S(1)}, u32[]{:S(2)}, u32[]{:S(2)}) collective-permute-start(f32[64,768]{1,0:T(8,128)S(1)} %pad_maximum_fusion.6), channel_id=1, source_target_pairs={{0,8},{1,9},{2,10},{3,11},{4,12},{5,13},{6,14},{7,15}} | collective-permute-start | bytes 589832 | tf_op jit(solution)/shard_map/ppermute | solution.py:349
  201.0 1.7 copy-start.8
  201.0 22.6 %copy-start.7 = (f32[4,64,256]{2,1,0:T(8,128)S(1)}, f32[4,64,256]{2,1,0:T(8,128)}, u32[]{:S(2)}) copy-start(f32[4,64,256]{2,1,0:T(8,128)} %copy-done.6) | copy-start | bytes 786436
  201.0 1.6 collective-permute-start.21
  202.7 6.2 %collective-permute-start.22 = (f32[64,256]{1,0:T(8,128)S(1)}, f32[64,256]{1,0:T(8,128)S(1)}, u32[]{:S(2)}, u32[]{:S(2)}) collective-permute-start(f32[64,256]{1,0:T(8,128)S(1)} %get-tuple-element.62), channel_id=1, source_target_pairs={{0,2},{1,3},{2,4},{3,5},{4,6},{5,7},{6,0},{7,1},{8,10},{9,11},{10,... | collective-permute-start | bytes 196616 | tf_op jit(solution)/shard_map/ppermute | solution.py:291
  204.3 5.3 %collective-permute-start.24 = (f32[64,256]{1,0:T(8,128)S(1)}, f32[64,256]{1,0:T(8,128)S(1)}, u32[]{:S(2)}, u32[]{:S(2)}) collective-permute-start(f32[64,256]{1,0:T(8,128)S(1)} %get-tuple-element.63), channel_id=1, source_target_pairs={{0,6},{1,7},{2,0},{3,1},{4,2},{5,3},{6,4},{7,5},{8,14},{9,15},{10,... | collective-permute-start | bytes 196616 | tf_op jit(solution)/shard_map/ppermute | solution.py:291
  206.5 6.4 %collective-permute-start.23 = (f32[64,256]{1,0:T(8,128)S(1)}, f32[64,256]{1,0:T(8,128)S(1)}, u32[]{:S(2)}, u32[]{:S(2)}) collective-permute-start(f32[64,256]{1,0:T(8,128)S(1)} %get-tuple-element.64), channel_id=1, source_target_pairs={{0,4},{1,5},{2,6},{3,7},{4,0},{5,1},{6,2},{7,3},{8,12},{9,13},{10,... | collective-permute-start | bytes 196616 | tf_op jit(solution)/shard_map/ppermute | solution.py:291
  212.9 4.8 %collective-permute-start.28 = (f32[64,256]{1,0:T(8,128)S(1)}, f32[64,256]{1,0:T(8,128)S(1)}, u32[]{:S(2)}, u32[]{:S(2)}) collective-permute-start(f32[64,256]{1,0:T(8,128)S(1)} %fusion.5), channel_id=1, source_target_pairs={{0,6},{1,7},{2,0},{3,1},{4,2},{5,3},{6,4},{7,5},{8,14},{9,15},{10,... | collective-permute-start | bytes 196616 | tf_op jit(solution)/shard_map/ppermute | solution.py:291
  215.2 6.7 %collective-permute-start.27 = (f32[64,256]{1,0:T(8,128)S(1)}, f32[64,256]{1,0:T(8,128)S(1)}, u32[]{:S(2)}, u32[]{:S(2)}) collective-permute-start(f32[64,256]{1,0:T(8,128)S(1)} %fusion.5), channel_id=1, source_target_pairs={{0,4},{1,5},{2,6},{3,7},{4,0},{5,1},{6,2},{7,3},{8,12},{9,13},{10,... | collective-permute-start | bytes 196616 | tf_op jit(solution)/shard_map/ppermute | solution.py:291
  215.2 6.7 %collective-permute-start.26 = (f32[64,256]{1,0:T(8,128)S(1)}, f32[64,256]{1,0:T(8,128)S(1)}, u32[]{:S(2)}, u32[]{:S(2)}) collective-permute-start(f32[64,256]{1,0:T(8,128)S(1)} %fusion.5), channel_id=1, source_target_pairs={{0,2},{1,3},{2,4},{3,5},{4,6},{5,7},{6,0},{7,1},{8,10},{9,11},{10,... | collective-permute-start | bytes 196616 | tf_op jit(solution)/shard_map/ppermute | solution.py:291
  215.8 6.1 %collective-permute-start.25 = (f32[64,256]{1,0:T(8,128)S(1)}, f32[64,256]{1,0:T(8,128)S(1)}, u32[]{:S(2)}, u32[]{:S(2)}) collective-permute-start(f32[64,256]{1,0:T(8,128)S(1)} %fusion.5), channel_id=1, source_target_pairs={{0,8},{1,9},{2,10},{3,11},{4,12},{5,13},{6,14},{7,15}} | collective-permute-start | bytes 196616 | tf_op jit(solution)/shard_map/ppermute | solution.py:358
  222.0 1.6 collective-permute-start.29
  222.3 2.3 copy-start.9
  225.3 1.4 collective-permute-start.30
  226.0 2.6 %collective-permute-start.31 = (f32[2,32,512]{2,1,0:T(8,128)S(1)}, f32[2,32,512]{2,1,0:T(8,128)S(1)}, u32[]{:S(2)}, u32[]{:S(2)}) collective-permute-start(f32[2,32,512]{2,1,0:T(8,128)S(1)} %get-tuple-element.51), channel_id=1, source_target_pairs={{8,16},{9,17},{10,18},{11,19},{12,20},{13,21},{14,22},{15,23}} | collective-permute-start | bytes 393224 | tf_op jit(solution)/shard_map/ppermute | solution.py:371
  227.1 13.4 %copy-start.3 = (f32[512,1024]{1,0:T(8,128)S(1)}, f32[512,1024]{1,0:T(8,128)}, u32[]{:S(2)}) copy-start(f32[512,1024]{1,0:T(8,128)} %all-reduce.3.cloned.1.call-done.value.refs_3_) | copy-start | bytes 6291460
  227.2 11.6 %collective-permute-start.32 = (f32[2,32,512]{2,1,0:T(8,128)S(1)}, f32[2,32,512]{2,1,0:T(8,128)S(1)}, u32[]{:S(2)}, u32[]{:S(2)}) collective-permute-start(f32[2,32,512]{2,1,0:T(8,128)S(1)} %get-tuple-element.53), channel_id=1, source_target_pairs={{16,24},{17,25},{18,26},{19,27},{20,28},{21,29},{22,30},{23,31}} | collective-permute-start | bytes 393224 | tf_op jit(solution)/shard_map/ppermute | solution.py:371
  229.1 11.5 %collective-permute-start.33 = (f32[2,32,512]{2,1,0:T(8,128)S(1)}, f32[2,32,512]{2,1,0:T(8,128)S(1)}, u32[]{:S(2)}, u32[]{:S(2)}) collective-permute-start(f32[2,32,512]{2,1,0:T(8,128)S(1)} %get-tuple-element.54), channel_id=1, source_target_pairs={{16,24},{17,25},{18,26},{19,27},{20,28},{21,29},{22,30},{23,31}} | collective-permute-start | bytes 393224 | tf_op jit(solution)/shard_map/ppermute | solution.py:371
Sparse Core Ops, SparseCore 0:
  35.8 66.3 all-reduce.2
